TPU v7x, 512 devices: a whole 4x4x16 slice. The times are simulated.
512 devices in a mesh: rows: 32 (over z_lo, y), cols: 16 (over x, z_hi, core).
Axes of the slice: x: 4, y: 4, z: 16 (z_hi: 2, z_lo: 8; z = z_hi * 8 + z_lo), core: 2. Of those that a mesh axis runs over, the one named last changes fastest.
Arguments:
- eigenvectors: float32 [2, 16384, 6144], P(None, 'rows', 'cols'), may hold values from -6 to 6
- reflectors: float32 [32, 4, 2, 512, 256], P('rows', None, None, 'cols'), may hold values from -0.1875 to 0.1875
- tri_factors: float32 [32, 4, 2, 256, 256], P('rows', None, None, 'cols'), may hold values from -0.1875 to 0.1875
- block_order: int32 [32, 4], P('rows'), may hold values from 0 to 3, each once within a row
Outputs:
- transformed: float32 [2, 16384, 6144], P(None, 'rows', 'cols')
Inputs may be any that keep to these rules, and one draw needn't show every extreme that they name: `block_order`: each row names the stored blocks 0 to 3 once each.
All inputs are finite; a program needn't handle non-finite values.
Results may differ from a plain program's by a relative error of at most 0.00011.
Values sent between devices are 32-bit elements; how exact they have to be, the bound alone decides.
A program may use at most 64 MiB of HBM per device.

v0:
```python
import jax
import jax.numpy as jnp
from jax import lax
from jax.experimental import pallas as pl
from jax.experimental.pallas import tpu as pltpu
from jax.sharding import PartitionSpec as P

MESH = pl.DeviceIdType.MESH
F32, BF16 = jnp.float32, jnp.bfloat16
ORDER = ((0, 0), (0, 1), (0, 2), (1, 0), (1, 1), (2, 0), (1, 2), (2, 1), (3, 0), (2, 2), (3, 1), (3, 2))


def split(a):
    hi = a.astype(BF16)
    return hi, (a - hi.astype(F32)).astype(BF16)


def make_kernel(sections, nx, ticks, win, band, lanes, chunks):
    half = win // 2
    vr = win // (4 * nx)
    fr = band // (4 * nx)

    def kernel(z_hbm, v_ref, f_ref, o_ref, out_hbm, got, zc, lifted, given, vt, vn, fn, bz, bw,
               in_sem, out_sem, zs, zr, xs, xr, ss, sr, ls, lr, rs, rr):
        r, c = lax.axis_index("rows"), lax.axis_index("cols")
        x, zh, k = c // 4, (c // 2) % 2, c % 2

        def slot(xx, zz, kk):
            return xx * 4 + zz * 2 + kk

        def at_x(d):
            return lax.rem(x + d + nx, nx)

        flip = slot(x, 1 - zh, k)
        sib = slot(x, zh, 1 - k)

        def remote(src, dst, s, rcv, dev):
            return pltpu.make_async_remote_copy(
                src_ref=src, dst_ref=dst, send_sem=s, recv_sem=rcv, device_id=dev, device_id_type=MESH)

        def zcopy(t):
            return remote(got.at[t, c], got.at[t, c], zs.at[t], zr.at[t], (r, flip))

        def xcopy(t, kind, d):
            s = slot(x, (zh, 1 - zh)[kind], k)
            return remote(got.at[t, s], got.at[t, s], xs.at[t, kind, d - 1], xr.at[t, kind, d - 1],
                          (r, slot(at_x(d), zh, k)))

        def scopy(t, kind, d):
            s = slot(at_x(-d), (zh, 1 - zh)[kind], k)
            m = kind * nx + d
            return remote(got.at[t, s], got.at[t, s], ss.at[t, m], sr.at[t, m], (r, sib))

        def heads(i, j):
            return zc.at[j, 0:half] if i == 0 else given.at[i - 1, j]

        def lift(i, j):
            return remote(heads(i, j), lifted.at[i, j], ls.at[i, j], lr.at[i, j], (r - 1, c))

        def give(i, j):
            return remote(lifted.at[i, j], given.at[i, j], rs.at[i, j], rr.at[i, j], (r + 1, c))

        barrier = pltpu.get_barrier_semaphore()
        partners = [(r, flip), (r, sib), (lax.rem(r + 1, sections), c), (lax.rem(r + sections - 1, sections), c)]
        partners += [(r, slot(at_x(d), zh, k)) for d in range(1, nx)]
        for dev in partners:
            pl.semaphore_signal(barrier, inc=1, device_id=dev, device_id_type=MESH)
        loads = []
        for j in range(chunks):
            for p in range(2):
                loads.append(pltpu.make_async_copy(
                    z_hbm.at[p, :, j * lanes:(j + 1) * lanes], zc.at[j, :, p * lanes:(p + 1) * lanes],
                    in_sem.at[2 * j + p]))
                loads[-1].start()
        for t in range(ticks):
            which = o_ref[0, t]
            got[t, c, :, 0:vr, :] = v_ref[0, which]
            got[t, c, :, vr:vr + fr, :] = f_ref[0, which]
        pl.semaphore_wait(barrier, len(partners))

        def own_out(t):
            zcopy(t).start()
            for d in range(1, nx):
                xcopy(t, 0, d).start()
            scopy(t, 0, 0).start()

        def own_in(t):
            for d in range(1, nx):
                xcopy(t, 0, d).wait_recv()
                scopy(t, 0, d).start()

        def flip_in(t):
            zcopy(t).wait_recv()
            for d in range(1, nx):
                xcopy(t, 1, d).start()
            scopy(t, 1, 0).start()

        def flip_on(t):
            for d in range(1, nx):
                xcopy(t, 1, d).wait_recv()
                scopy(t, 1, d).start()

        def all_in(t):
            for kind in range(2):
                for d in range(nx):
                    scopy(t, kind, d).wait_recv()

        def convert(t):
            for xx in range(nx):
                rows = 4 * vr
                at = xx * rows
                for p in range(2):
                    v = got[t, 4 * xx:4 * xx + 4, p, 0:vr, :].reshape(rows, band)
                    hi, lo = split(v)
                    vn[t, p * win + at:p * win + at + rows, 0:band] = hi
                    vn[t, p * win + at:p * win + at + rows, band:2 * band] = hi
                    vn[t, p * win + at:p * win + at + rows, 2 * band:3 * band] = lo
                    hi, lo = split(v.T)
                    vt[t, p * band:(p + 1) * band, at:at + rows] = hi
                    vt[t, p * band:(p + 1) * band, win + at:win + at + rows] = hi
                    vt[t, p * band:(p + 1) * band, 2 * win + at:2 * win + at + rows] = lo
            keep = lax.broadcasted_iota(jnp.int32, (band, band), 0) <= lax.broadcasted_iota(jnp.int32, (band, band), 1)
            for p in range(2):
                f = jnp.where(keep, got[t, :, p, vr:vr + fr, :].reshape(band, band), 0.0)
                hi, lo = split(f)
                fn[t, p * band:(p + 1) * band, 0:band] = hi
                fn[t, p * band:(p + 1) * band, band:2 * band] = hi
                fn[t, p * band:(p + 1) * band, 2 * band:3 * band] = lo

        def product(left, right, rows, conj):
            both = jnp.dot(left, right, preferred_element_type=F32)
            a, b = both[:rows], both[rows:]
            if conj:
                return jnp.concatenate([a[:, :lanes] + b[:, lanes:], a[:, lanes:] - b[:, :lanes]], axis=1)
            return jnp.concatenate([a[:, :lanes] - b[:, lanes:], a[:, lanes:] + b[:, :lanes]], axis=1)

        def apply(t, first, second):
            for n, ref in enumerate((first, second)):
                hi, lo = split(ref[...])
                bz[n * half:(n + 1) * half] = hi
                bz[win + n * half:win + (n + 1) * half] = lo
                bz[2 * win + n * half:2 * win + (n + 1) * half] = hi
            w = product(vt[t], bz[...], band, True)
            hi, lo = split(w)
            bw[0, 0:band], bw[0, band:2 * band], bw[0, 2 * band:3 * band] = hi, lo, hi
            u = product(fn[t], bw[0], band, False)
            hi, lo = split(u)
            bw[1, 0:band], bw[1, band:2 * band], bw[1, 2 * band:3 * band] = hi, lo, hi
            delta = product(vn[t], bw[1], win, False)
            first[...] = first[...] - delta[:half]
            second[...] = second[...] - delta[half:]

        def take(i, j):
            @pl.when(r > 0)
            def _():
                lift(i, j).wait_send()
                give(i, j).wait_recv()

            @pl.when(r == 0)
            def _():
                given[i, j] = heads(i, j)[...]

        def step(t, j):
            i = t // 2
            head, tail = heads(i, j), zc.at[j, half:win]
            if t % 2 == 0:
                if t == 0:
                    loads[2 * j].wait()
                    loads[2 * j + 1].wait()
                else:
                    take(i - 1, j)
                apply(t, head, tail)

                @pl.when(r > 0)
                def _():
                    lift(i, j).start()
            else:
                @pl.when(r < sections - 1)
                def _():
                    lift(i, j).wait_recv()
                    apply(t, tail, lifted.at[i, j])
                    give(i, j).start()

        def stores(j, part):
            rows = slice(part * half, (part + 1) * half)
            ref = zc.at[j, half:win] if part else heads(ticks // 2, j)
            return [pltpu.make_async_copy(
                ref.at[:, p * lanes:(p + 1) * lanes], out_hbm.at[p, rows, j * lanes:(j + 1) * lanes],
                out_sem.at[part, 2 * j + p]) for p in range(2)]

        def gathered(t):
            flip_on(t)
            all_in(t)
            convert(t)

        def pending(t):
            zcopy(t).wait_send()
            own_out(t + 1)

        own_out(0)
        own_in(0)
        pending(0)
        flip_in(0)
        gathered(0)
        done = set([0])
        for n, (t, j) in enumerate(ORDER):
            if t not in done:
                if t == 1:
                    own_in(1)
                    pending(1)
                    flip_in(1)
                gathered(t)
                done.add(t)
            step(t, j)
            if (t, j) == (1, 0):
                own_in(2)
                pending(2)
            if (t, j) == (1, 1):
                flip_in(2)
            if (t, j) == (2, 0):
                own_in(3)
            if (t, j) == (2, 1):
                flip_in(3)
            if t == ticks - 1:
                for copy in stores(j, 1):
                    copy.start()
        last = ticks // 2 - 1
        for j in range(chunks):
            take(last, j)
            for copy in stores(j, 0):
                copy.start()
        zcopy(ticks - 1).wait_send()
        for t in range(ticks):
            for kind in range(2):
                for d in range(nx):
                    if d:
                        xcopy(t, kind, d).wait_send()
                    scopy(t, kind, d).wait_send()

        @pl.when(r < sections - 1)
        def _():
            for i in range(ticks // 2):
                for j in range(chunks):
                    give(i, j).wait_send()
        for j in range(chunks):
            for part in range(2):
                for copy in stores(j, part):
                    copy.wait()

    return kernel


def solution(mesh):
    sections, cols = mesh.shape["rows"], mesh.shape["cols"]
    nx = cols // 4

    def shards(eigenvectors, reflectors, tri_factors, block_order):
        ticks, band = reflectors.shape[1], reflectors.shape[4]
        win = reflectors.shape[3] * cols
        lanes = 128
        chunks = eigenvectors.shape[2] // lanes
        half = win // 2
        dma = pltpu.SemaphoreType.DMA
        return pl.pallas_call(
            make_kernel(sections, nx, ticks, win, band, lanes, chunks),
            out_shape=jax.ShapeDtypeStruct(eigenvectors.shape, F32),
            in_specs=[
                pl.BlockSpec(memory_space=pl.ANY),
                pl.BlockSpec(memory_space=pltpu.VMEM),
                pl.BlockSpec(memory_space=pltpu.VMEM),
                pl.BlockSpec(memory_space=pltpu.SMEM),
            ],
            out_specs=pl.BlockSpec(memory_space=pl.ANY),
            scratch_shapes=[
                pltpu.VMEM((ticks, cols, 2, (win + band) // cols, band), F32),
                pltpu.VMEM((chunks, win, 2 * lanes), F32),
                pltpu.VMEM((ticks // 2, chunks, half, 2 * lanes), F32),
                pltpu.VMEM((ticks // 2, chunks, half, 2 * lanes), F32),
                pltpu.VMEM((ticks, 2 * band, 3 * win), BF16),
                pltpu.VMEM((ticks, 2 * win, 3 * band), BF16),
                pltpu.VMEM((ticks, 2 * band, 3 * band), BF16),
                pltpu.VMEM((3 * win, 2 * lanes), BF16),
                pltpu.VMEM((2, 3 * band, 2 * lanes), BF16),
                dma((2 * chunks,)),
                dma((2, 2 * chunks)),
                dma((ticks,)),
                dma((ticks,)),
                dma((ticks, 2, max(nx - 1, 1))),
                dma((ticks, 2, max(nx - 1, 1))),
                dma((ticks, 2 * nx)),
                dma((ticks, 2 * nx)),
                dma((ticks // 2, chunks)),
                dma((ticks // 2, chunks)),
                dma((ticks // 2, chunks)),
                dma((ticks // 2, chunks)),
            ],
            compiler_params=pltpu.CompilerParams(
                collective_id=0, has_side_effects=True, vmem_limit_bytes=60 * 2**20),
            name="sweep",
        )(eigenvectors, reflectors, tri_factors, block_order)

    return jax.shard_map(
        shards,
        mesh=mesh,
        in_specs=(
            P(None, "rows", "cols"),
            P("rows", None, None, "cols", None),
            P("rows", None, None, "cols", None),
            P("rows", None),
        ),
        out_specs=P(None, "rows", "cols"),
        check_vma=False,
    )
```

profile of v0, /device:TPU:32, one launch (start us, length us, event | category | flops | bytes accessed | tf_op | source)
XLA Modules:
  0.0 131.7 jit_solution(934008547702472471)
XLA Ops:
  0.0 129.0 %sweep.1 = f32[2,512,384]{2,1,0:T(8,128)} custom-call(f32[2,512,384]{2,1,0:T(8,128)} %z_hbm.1, f32[1,4,2,32,256]{4,3,2,1,0:T(8,128)} %v_ref.1, f32[1,4,2,16,256]{4,3,2,1,0:T(8,128)} %f_ref.1, s32[1,4]{1,0:T(1,128)} %o_ref.1), custom_call_target="tpu_custom_call" | custom-call | tf_op jit(solution)/shard_map/sweep/pallas_call | solution.py:264
  129.1 2.7 %copy.6 = f32[2,512,384]{2,1,0:T(8,128)} copy(f32[2,512,384]{2,1,0:T(8,128)} %sweep.1) | data formatting | bytes 3145728
where the time goes:
time: 132 us
  Pallas kernels  129 us (98%)
  local copies, waits for them, and re-layouts  2.65 us (2%)
    pallas_call x1, Pallas kernels, shards(): pl.pallas_call(make_kernel(sections, nx, ticks, win, band, lanes, chunks)...  129 us
    unnamed x1, local copies, waits for them, and re-layouts  2.65 us

commit v1 on v0

--- a/solution.py
+++ b/solution.py
@@ -7,7 +7,11 @@
 
 MESH = pl.DeviceIdType.MESH
 F32, BF16 = jnp.float32, jnp.bfloat16
-ORDER = ((0, 0), (0, 1), (0, 2), (1, 0), (1, 1), (2, 0), (1, 2), (2, 1), (3, 0), (2, 2), (3, 1), (3, 2))
+SCHEDULE = (
+    "Z0", "X0", "Z1", "O0", "X1", "F0", "Z2", "O1", "G0", "X2", "A0", "S00", "F1", "Z3",
+    "S01", "O2", "S02", "G1", "X3", "A1", "S10", "F2", "O3", "S11", "G2", "A2", "S20", "F3",
+    "S12", "S21", "G3", "A3", "S30", "S22", "S31", "S32",
+)
 
 
 def split(a):
@@ -79,7 +83,6 @@
         pl.semaphore_wait(barrier, len(partners))
 
         def own_out(t):
-            zcopy(t).start()
             for d in range(1, nx):
                 xcopy(t, 0, d).start()
             scopy(t, 0, 0).start()
@@ -127,28 +130,30 @@
                 fn[t, p * band:(p + 1) * band, band:2 * band] = hi
                 fn[t, p * band:(p + 1) * band, 2 * band:3 * band] = lo
 
-        def product(left, right, rows, conj):
-            both = jnp.dot(left, right, preferred_element_type=F32)
-            a, b = both[:rows], both[rows:]
+        def product(left, rows, m, right, conj):
+            a = jnp.dot(left[m * lanes:(m + 1) * lanes, :], right, preferred_element_type=F32)
+            b = jnp.dot(left[rows + m * lanes:rows + (m + 1) * lanes, :], right, preferred_element_type=F32)
             if conj:
                 return jnp.concatenate([a[:, :lanes] + b[:, lanes:], a[:, lanes:] - b[:, :lanes]], axis=1)
             return jnp.concatenate([a[:, :lanes] - b[:, lanes:], a[:, lanes:] + b[:, :lanes]], axis=1)
 
+        def put(n, m, w):
+            hi, lo = split(w)
+            for q, part in enumerate((hi, lo, hi)):
+                bw[n, q * band + m * lanes:q * band + (m + 1) * lanes] = part
+
         def apply(t, first, second):
             for n, ref in enumerate((first, second)):
                 hi, lo = split(ref[...])
-                bz[n * half:(n + 1) * half] = hi
-                bz[win + n * half:win + (n + 1) * half] = lo
-                bz[2 * win + n * half:2 * win + (n + 1) * half] = hi
-            w = product(vt[t], bz[...], band, True)
-            hi, lo = split(w)
-            bw[0, 0:band], bw[0, band:2 * band], bw[0, 2 * band:3 * band] = hi, lo, hi
-            u = product(fn[t], bw[0], band, False)
-            hi, lo = split(u)
-            bw[1, 0:band], bw[1, band:2 * band], bw[1, 2 * band:3 * band] = hi, lo, hi
-            delta = product(vn[t], bw[1], win, False)
-            first[...] = first[...] - delta[:half]
-            second[...] = second[...] - delta[half:]
+                for q, part in enumerate((hi, lo, hi)):
+                    bz[q * win + n * half:q * win + (n + 1) * half] = part
+            for m in range(band // lanes):
+                put(0, m, product(vt.at[t], band, m, bz[...], True))
+            for m in range(band // lanes):
+                put(1, m, product(fn.at[t], band, m, bw[0], False))
+            for m in range(win // lanes):
+                ref, at = (first, m * lanes) if m * lanes < half else (second, m * lanes - half)
+                ref[at:at + lanes, :] = ref[at:at + lanes, :] - product(vn.at[t], win, m, bw[1], False)
 
         def take(i, j):
             @pl.when(r > 0)
@@ -188,49 +193,27 @@
                 ref.at[:, p * lanes:(p + 1) * lanes], out_hbm.at[p, rows, j * lanes:(j + 1) * lanes],
                 out_sem.at[part, 2 * j + p]) for p in range(2)]
 
-        def gathered(t):
-            flip_on(t)
+        def ready(t):
             all_in(t)
             convert(t)
 
-        def pending(t):
-            zcopy(t).wait_send()
-            own_out(t + 1)
-
-        own_out(0)
-        own_in(0)
-        pending(0)
-        flip_in(0)
-        gathered(0)
-        done = set([0])
-        for n, (t, j) in enumerate(ORDER):
-            if t not in done:
-                if t == 1:
-                    own_in(1)
-                    pending(1)
-                    flip_in(1)
-                gathered(t)
-                done.add(t)
-            step(t, j)
-            if (t, j) == (1, 0):
-                own_in(2)
-                pending(2)
-            if (t, j) == (1, 1):
-                flip_in(2)
-            if (t, j) == (2, 0):
-                own_in(3)
-            if (t, j) == (2, 1):
-                flip_in(3)
-            if t == ticks - 1:
-                for copy in stores(j, 1):
-                    copy.start()
+        ops = dict(Z=lambda t: zcopy(t).start(), X=own_out, O=own_in, F=flip_in, G=flip_on, A=ready)
+        for item in SCHEDULE:
+            if item[0] == "S":
+                t, j = int(item[1]), int(item[2])
+                step(t, j)
+                if t == ticks - 1:
+                    for copy in stores(j, 1):
+                        copy.start()
+            else:
+                ops[item[0]](int(item[1]))
         last = ticks // 2 - 1
         for j in range(chunks):
             take(last, j)
             for copy in stores(j, 0):
                 copy.start()
-        zcopy(ticks - 1).wait_send()
         for t in range(ticks):
+            zcopy(t).wait_send()
             for kind in range(2):
                 for d in range(nx):
                     if d:

time: 132 us -> 106 us (0.80)
  the two profiles are of different devices: /device:TPU:32 before, /device:TPU:8 now
where the time goes in v1:
time: 106 us
  Pallas kernels  104 us (98%)
  local copies, waits for them, and re-layouts  2.65 us (2%)
    pallas_call x1, Pallas kernels, shards(): pl.pallas_call(make_kernel(sections, nx, ticks, win, band, lanes, chunks)...  104 us
    unnamed x1, local copies, waits for them, and re-layouts  2.65 us

profile of v1, /device:TPU:8, one launch (start us, length us, event | category | flops | bytes accessed | tf_op | source)
XLA Modules:
  0.0 106.3 jit_solution(11268042217095646304)
XLA Ops:
  0.0 103.6 %sweep.1 = f32[2,512,384]{2,1,0:T(8,128)} custom-call(f32[2,512,384]{2,1,0:T(8,128)} %z_hbm.1, f32[1,4,2,32,256]{4,3,2,1,0:T(8,128)} %v_ref.1, f32[1,4,2,16,256]{4,3,2,1,0:T(8,128)} %f_ref.1, s32[1,4]{1,0:T(1,128)} %o_ref.1), custom_call_target="tpu_custom_call" | custom-call | tf_op jit(solution)/shard_map/sweep/pallas_call | solution.py:247
  103.7 2.7 %copy.6 = f32[2,512,384]{2,1,0:T(8,128)} copy(f32[2,512,384]{2,1,0:T(8,128)} %sweep.1) | data formatting | bytes 3145728
